TPU v7x, 256 devices: a whole 4x4x8 slice. The times are simulated.
256 devices in a mesh: row: 32 (over z, x), col: 8 (over y, core).
Axes of the slice: x: 4, y: 4, z: 8, core: 2. Of those that a mesh axis runs over, the one named last changes fastest.
Arguments:
- activations: bfloat16 [4096, 26624], P('col', 'row'), may hold values from -6 to 6
- d_out: bfloat16 [4096, 8192], P('row', 'col'), may hold values from -60 to 60
- levels: bfloat16 [26624, 8192], P('row', 'col'), may hold values from -6 to 6
- scales: float32 [8192], P('col'), may hold values from 0.002 to 0.02
- clip_mask: int32 [26624, 8192], P('row', 'col'), may hold values 0 or 1
Outputs:
- d_in: float32 [4096, 26624], P('col', 'row')
- d_levels: float32 [26624, 8192], P('row', 'col')
All inputs are finite; a program needn't handle non-finite values. Where the computation divides by a largest or mean magnitude, that divisor is 1e-20 or more. No bound on the sum of `clip_mask` on one device may be relied on, other than what follows from the above.
Results may differ from a plain program's by a relative error of at most 0.004.
Values may be sent and summed in bfloat16 or wider, within the bound.
A program may use at most 128 MiB of HBM per device.

v0:
```python
import jax
import jax.numpy as jnp
from jax import lax
from jax.sharding import PartitionSpec as P

peak_level = 4.0
eps = 1e-06


def on_device(activations, d_out, levels, scales, clip_mask):
    raw_all = lax.all_gather(d_out, "row", axis=0, tiled=True).astype(jnp.float32)
    block_peak = jnp.max(jnp.abs(raw_all))
    amax = lax.pmax(block_peak, "col")
    quant_all = (raw_all * (peak_level / (amax + eps))).astype(jnp.bfloat16)
    dequant = (levels.astype(jnp.float32) * scales[None, :]).astype(jnp.bfloat16)
    grad_rows = quant_all
    product = lax.dot_general(
        lax.all_gather(activations, "col", axis=0, tiled=True),
        grad_rows,
        (((0,), (0,)), ((), ())),
        preferred_element_type=jnp.float32,
    )
    d_levels = clip_mask.astype(jnp.float32) * scales[None, :] * product
    grad_rows = quant_all
    d_in = lax.psum_scatter(
        lax.dot_general(
            grad_rows, dequant, (((1,), (1,)), ((), ())), preferred_element_type=jnp.float32
        ),
        "col",
        scatter_dimension=0,
        tiled=True,
    )
    return (d_in, d_levels)


def solution(mesh):
    placed = (P("col", "row"), P("row", "col"), P("row", "col"), P("col"), P("row", "col"))
    return jax.shard_map(
        on_device,
        mesh=mesh,
        in_specs=placed,
        out_specs=(P("col", "row"), P("row", "col")),
        check_vma=False,
    )
```

profile of v0, /device:TPU:16, one launch (start us, length us, event | category | flops | bytes accessed | tf_op | source)
XLA Modules:
  0.0 243.9 jit_solution(14397366424709708019)
XLA Ops:
  7.2 0.0 copy-start.1
  7.2 0.0 copy-start.2
  7.2 0.0 all-gather.3.cloned.1.call-start
  7.2 0.7 all-gather.3.cloned.1.call-update
  7.9 0.0 all-gather.5.cloned.1.call-start
  8.0 0.7 all-gather.5.cloned.1.call-update
  8.7 0.0 reduce-scatter.2.cloned.1.call-start
  8.7 103.0 %all-gather.3.cloned.1.call-done = bf16[4096,1024]{1,0:T(8,128)(2,1)} async-done(((bf16[128,1024]{1,0:T(8,128)(2,1)}), bf16[4096,1024]{1,0:T(8,128)(2,1)}) %all-gather.3.cloned.1.call-update) | async-done | bytes 8388624 | tf_op jit(solution)/shard_map/all_gather | solution.py:11
  111.7 6.0 %fusion = f32[]{:T(128)} fusion(bf16[4096,1024]{1,0:T(8,128)(2,1)} %all-gather.3.cloned.1.call-done), kind=kLoop, calls=%fused_computation.2 | loop fusion | flops 12582911 | bytes 8388612 | tf_op jit(solution)/shard_map/reduce_max | solution.py:12
  117.8 11.3 %pmax.7 = f32[]{:T(128)} all-reduce(f32[]{:T(128)} %fusion), channel_id=1, replica_groups=mesh['row'=32,'col'=8] {'col'}, use_global_device_ids=true, to_apply=%region_1.0 | all-reduce | flops 1 | bytes 8 | tf_op jit(solution)/shard_map/pmax | solution.py:13
  129.8 0.0 copy-done.1
  129.8 0.0 copy-done.2
  129.8 13.9 %fusion.4 = f32[4096,832]{0,1:T(8,128)} fusion(bf16[4096,1024]{1,0:T(8,128)(2,1)} %all-gather.3.cloned.1.call-done, f32[]{:T(128)S(6)} %div.3, bf16[832,1024]{1,0:T(8,128)(2,1)S(1)} %copy-done.1, f32[1024]{0:T(1024)S(1)} %copy-done.2), kind=kOutput, calls=%fused_computation.5 | convolution fusion | flops 6994460672 | bytes 23728132 | tf_op jit(solution)/shard_map/dot_general | solution.py:26
  143.7 0.0 copy-start
  143.7 0.0 reduce-scatter.2.cloned.1.call-update
  143.7 11.6 %all-gather.5.cloned.1.call-done = bf16[4096,832]{0,1:T(8,128)(2,1)} async-done(((bf16[512,832]{0,1:T(8,128)(2,1)}), bf16[4096,832]{0,1:T(8,128)(2,1)}) %all-gather.5.cloned.1.call-update) | async-done | bytes 6815760 | tf_op jit(solution)/shard_map/all_gather | solution.py:18
  155.3 0.0 copy-done
  155.3 12.8 %bitcast_multiply_fusion = f32[832,1024]{1,0:T(8,128)} fusion(s32[832,1024]{1,0:T(8,128)S(1)} %copy-done, bf16[4096,832]{0,1:T(8,128)(2,1)} %all-gather.5.cloned.1.call-done, bf16[4096,1024]{1,0:T(8,128)(2,1)} %all-gather.3.cloned.1.call-done, f32[]{:T(128)S(6)} %div.3, f32[1024]{0:T(1024)S(1)} %copy-done.2), kind=kOutput, calls=%fused_computation.6 | convolution fusion | flops 6994460672 | bytes 22024196 | tf_op jit(solution)/shard_map/dot_general | solution.py:17
  168.1 69.4 %reduce-scatter.2.cloned.1.call-done = f32[512,832]{0,1:T(8,128)} async-done(((f32[4096,832]{0,1:T(8,128)}), f32[512,832]{0,1:T(8,128)}) %reduce-scatter.2.cloned.1.call-update) | async-done | bytes 1703952 | tf_op jit(solution)/shard_map/reduce_scatter | solution.py:25
Async XLA Ops:
  7.2 122.6 %copy-start.1 = (bf16[832,1024]{1,0:T(8,128)(2,1)S(1)}, bf16[832,1024]{1,0:T(8,128)(2,1)}, u32[]{:S(2)}) copy-start(bf16[832,1024]{1,0:T(8,128)(2,1)} %param.7) | copy-start | bytes 5111812
  7.2 122.6 %copy-start.2 = (f32[1024]{0:T(1024)S(1)}, f32[1024]{0:T(1024)}, u32[]{:S(2)}) copy-start(f32[1024]{0:T(1024)} %param.8) | copy-start | bytes 12292
  7.2 104.6 %all-gather.3.cloned.1.call-start = ((), (), s32[]{:S(2)}) async-start(), calls=%async_computation.1 | async-start | bytes 8650752 | tf_op jit(solution)/shard_map/all_gather | solution.py:11
  7.9 147.3 %all-gather.5.cloned.1.call-start = ((), (), s32[]{:S(2)}) async-start(), calls=%async_computation.3 | async-start | bytes 7667712 | tf_op jit(solution)/shard_map/all_gather | solution.py:18
  8.7 228.7 %reduce-scatter.2.cloned.1.call-start = ((), (), s32[]{:S(2)}) async-start(), calls=%async_computation.2 | async-start | bytes 15335424 | tf_op jit(solution)/shard_map/reduce_scatter | solution.py:25
  143.7 11.6 %copy-start = (s32[832,1024]{1,0:T(8,128)S(1)}, s32[832,1024]{1,0:T(8,128)}, u32[]{:S(2)}) copy-start(s32[832,1024]{1,0:T(8,128)} %param.9) | copy-start | bytes 10223620
Sparse Core Ops, SparseCore 0:
  10.6 101.0 all-gather.2
  113.6 41.6 all-gather.4
  158.4 78.9 reduce-scatter.1
where the time goes:
time: 247 us; the launch traced here: 244 us
  waiting for transfers between devices  185 us (75%)
  matrix products  26.6 us (11%)
  between operations  14.5 us (6%)
  blocking collectives  11.3 us (5%)
  other arithmetic  6.03 us (2%)
    all_gather x1, waiting for transfers between devices, on_device(): lax.all_gather(d_out, 'row', axis=0, tiled=True).astype(jnp.float32)  103 us
    reduce_scatter x1, waiting for transfers between devices, on_device(): lax.psum_scatter(lax.dot_general(grad_rows, dequant, (((1,), (1,)), ((),...  69.4 us
    dot_general x1, matrix products, on_device(): lax.dot_general(grad_rows, dequant, (((1,), (1,)), ((), ())), preferred_e...  13.9 us
    dot_general x1, matrix products, on_device(): lax.dot_general(lax.all_gather(activations, 'col', axis=0, tiled=True), g...  12.8 us
    all_gather x1, waiting for transfers between devices, on_device(): lax.all_gather(activations, 'col', axis=0, tiled=True)  11.6 us
    pmax x1, blocking collectives, on_device(): amax = lax.pmax(block_peak, 'col')  11.3 us
    reduce_max x1, other arithmetic, on_device(): block_peak = jnp.max(jnp.abs(raw_all))  6.03 us
  transfers between devices with their start and end apart: 3, of which 3 were waited for; matrix products, arithmetic and copies ran while one was open for 13% of the time, Pallas kernels for 0%

commit v1 on v0

v1 whole, which is shorter than its diff:
```python
import jax
import jax.numpy as jnp
from jax import lax
from jax.experimental import pallas as pl
from jax.experimental.pallas import tpu as pltpu
from jax.sharding import PartitionSpec as P

peak_level = 4.0
eps = 1e-06

MESH = pl.DeviceIdType.MESH
NT = (((1,), (1,)), ((), ()))
NN = (((1,), (0,)), ((), ()))
F32 = jnp.float32
BF16 = jnp.bfloat16

K = 832
T = 512
C = 1024
XF = 48
HALF = K // 2
LO = pl.ds(0, HALF)
HI = pl.ds(HALF, HALF)
CH = 208
N_EV = 96

OFFS = (0, 1, 7, 2, 6, 3, 5, 4)


def up(h):
    return 2 * h - 1


def down(h):
    return 7 if h == 4 else 2 * h


def kernel(act, dout, levels, scales, mask, din_out, dlev_out,
           D, A, W, acc, Cs, Ssend, Srecv, Y, rel, fin, lev_v, mask_v, mx, Mx,
           ss, rs, ls):
    row, col = lax.axis_index("row"), lax.axis_index("col")
    z, x = row // 4, row % 4
    y, k = col // 2, col % 2

    def dev(dz=0, dx=0, dy=0, dk=0):
        return (((z + dz) % 8) * 4 + (x + dx) % 4, ((y + dy) % 4) * 2 + (k + dk) % 2)

    zp, zm, xp, xm, xx = dev(dz=1), dev(dz=7), dev(dx=1), dev(dx=3), dev(dx=2)
    yp, ym, yy, kk = dev(dy=1), dev(dy=3), dev(dy=2), dev(dk=1)

    ev = {}

    def plan(name, src, dst, to):
        ev[name] = (len(ev), src, dst, to)

    def copy_of(name):
        i, src, dst, to = ev[name]
        return pltpu.make_async_remote_copy(
            src_ref=src, dst_ref=dst, send_sem=ss.at[i], recv_sem=rs.at[i],
            device_id=to, device_id_type=MESH)

    def send(name, *what):
        if what:
            plan(name, *what)
        copy_of(name).start()

    def got(*names):
        for n in names:
            copy_of(n).wait_recv()

    plan("relL", Y.at[2, LO], rel.at[0], yp)
    plan("relU", Y.at[2, HI], rel.at[1], ym)
    plan("fmU", Y.at[0, HI], fin.at[0, HI], yp)
    plan("fmL", Y.at[0, LO], fin.at[0, LO], yp)
    plan("fpU", Y.at[1, HI], fin.at[1, HI], ym)
    plan("fpL", Y.at[1, LO], fin.at[1, LO], ym)
    for s in range(8):
        d = ((z + OFFS[s]) % 8 // 2 + 4 - y) % 4
        plan(f"sib{s}", Ssend.at[d], Srecv.at[d], kk)

    own = 2 * y + k
    l_d = pltpu.make_async_copy(dout, D.at[0, x], ls.at[0])
    l_a = pltpu.make_async_copy(act, A.at[own], ls.at[1])
    l_w = pltpu.make_async_copy(levels, lev_v, ls.at[2])
    l_m = pltpu.make_async_copy(mask, mask_v, ls.at[3])

    barrier = pltpu.get_barrier_semaphore()
    peers = (zp, zm, xp, xm, xx, yp, ym, yy, kk)
    for p in peers:
        pl.semaphore_signal(barrier, inc=1, device_id=p, device_id_type=MESH)
    l_d.start()
    l_w.start()
    l_a.start()
    pl.semaphore_wait(barrier, len(peers))

    a_rows, b_rows = pl.ds(0, XF), pl.ds(XF, 128 - XF)
    b_lo, b_hi = pl.ds(XF, 48), pl.ds(XF + 48, 80 - 48)

    send("xA+", dout.at[a_rows], D.at[0, x, a_rows], xp)
    send("xA-", dout.at[a_rows], D.at[0, x, a_rows], xm)
    send("zB+1", dout.at[b_rows], D.at[down(1), x, b_rows], zp)
    send("zB-1", dout.at[b_rows], D.at[up(1), x, b_rows], zm)
    send("xA2", dout.at[a_rows], D.at[0, x, a_rows], xx)
    send("aL+", act.at[LO], A.at[own, LO], yp)
    send("aU-", act.at[HI], A.at[own, HI], ym)
    send("xB+0", dout.at[b_rows], D.at[0, x, b_rows], xp)
    send("xB-0", dout.at[b_rows], D.at[0, x, b_rows], xm)
    send("aU+", act.at[HI], A.at[own, HI], yp)
    send("aL-", act.at[LO], A.at[own, LO], ym)
    send("ak0", act, A.at[own], kk)
    l_m.start()

    l_w.wait()

    def deq(i, _):
        r = pl.multiple_of(i * CH, 16)
        W[pl.ds(r, CH), :] = (lev_v[pl.ds(r, CH), :].astype(F32) * scales[...]).astype(BF16)
        return 0

    lax.fori_loop(0, K // CH, deq, 0)
    mx[...] = jnp.zeros_like(mx)
    l_d.wait()

    def fwd_z(h):
        got(f"zB+{h}", f"zB-{h}")
        if h < 3:
            send(f"zB+{h+1}", D.at[down(h), x, b_rows], D.at[down(h + 1), x, b_rows], zp)
            send(f"zB-{h+1}", D.at[up(h), x, b_rows], D.at[up(h + 1), x, b_rows], zm)
        if h == 3:
            send("zB+4", D.at[down(3), x, b_lo], D.at[7, x, b_lo], zp)
            send("zB-4", D.at[up(3), x, b_hi], D.at[7, x, b_hi], zm)
        if h < 4:
            pair = D.at[pl.ds(2 * h - 1, 2), x, b_rows]
        else:
            pair = D.at[7, x, b_rows]
        send(f"xB+{h}", pair, pair, xp)
        send(f"xB-{h}", pair, pair, xm)

    def fwd_a(h):
        if h == 0:
            got("xA+", "xA-", "xA2")
        elif h < 4:
            got(f"zA0+{h}", f"zA0-{h}", f"zA1+{h}", f"zA1-{h}")
        else:
            got("zA0+4", "zA1-4")
            return
        lo, hi = (0, 0) if h == 0 else (down(h), up(h))
        for j in range(2):
            xs = pl.ds(2 * j, 2)
            if h < 3 or j == 0:
                send(f"zA{j}+{h+1}", D.at[lo, xs, a_rows], D.at[down(h + 1), xs, a_rows], zp)
            if h < 3 or j == 1:
                send(f"zA{j}-{h+1}", D.at[hi, xs, a_rows], D.at[up(h + 1) if h < 3 else 7, xs, a_rows], zm)

    xl, xr = (x + 3) % 4, (x + 1) % 4

    def relay_x(h):
        got(f"xB+{h}", f"xB-{h}")
        if h in (0, 4):
            s = 0 if h == 0 else 7
            r0, r1 = D.at[s, xl, b_lo], D.at[s, xr, b_hi]
        else:
            r0, r1 = D.at[up(h), xl, b_rows], D.at[down(h), xr, b_rows]
        send(f"xr+{h}", r0, r0, xp)
        send(f"xr-{h}", r1, r1, xm)

    def relayed_x(h):
        got(f"xr+{h}", f"xr-{h}")

    def where(s):
        b = (z + OFFS[s]) % 8
        return b, b % 2 == k, (b // 2 + 4 - y) % 4

    def mm1(s):
        b, mine, d = where(s)

        def part():
            return lax.dot_general(W[...], D[s].reshape(T, C), NT, preferred_element_type=F32)

        @pl.when(mine)
        def _():
            Cs[d] = part()

        @pl.when(jnp.logical_not(mine))
        def _():
            Ssend[d] = part().astype(BF16)
            send(f"sib{s}")

        def big(i, m):
            r = pl.multiple_of(i * 16, 16)
            return jnp.maximum(m, jnp.abs(Dm[s, pl.ds(r, 16), :]))

        Dm = D.reshape(8, T, C)
        mx[...] = lax.fori_loop(0, T // 16, big, mx[...], unroll=4)

    def rows_of(lo, n, fn):
        def body(i, _):
            fn(pl.ds(pl.multiple_of(lo + i * CH, 16), CH))
            return 0
        lax.fori_loop(0, n // CH, body, 0)

    def pair_sum(d, r):
        return Cs[d, r, :] + Srecv[d, r, :].astype(F32)

    def stage2(s):
        b, mine, d = where(s)

        @pl.when(mine)
        def _():
            got(f"sib{s}")

            @pl.when(d == 2)
            def _():
                def f(r):
                    Y[2, r, :] = pair_sum(2, r).astype(BF16)
                rows_of(0, K, f)
                send("relL")
                send("relU")

            @pl.when(d == 1)
            def _():
                def f(r):
                    Y[0, r, :] = pair_sum(1, r).astype(BF16)
                rows_of(HALF, HALF, f)
                send("fmU")

            @pl.when(d == 3)
            def _():
                def f(r):
                    Y[1, r, :] = pair_sum(3, r).astype(BF16)
                rows_of(0, HALF, f)
                send("fpL")

    def stage3(s):
        b, mine, d = where(s)

        @pl.when(jnp.logical_and(mine, d == 1))
        def _():
            got("relL")

            def f(r):
                Y[0, r, :] = (pair_sum(1, r) + rel[0, r, :].astype(F32)).astype(BF16)
            rows_of(0, HALF, f)
            send("fmL")

        @pl.when(jnp.logical_and(mine, d == 3))
        def _():
            got("relU")

            def f(i, _):
                r = pl.ds(pl.multiple_of(HALF + i * CH, 16), CH)
                q = pl.ds(pl.multiple_of(i * CH, 16), CH)
                Y[1, r, :] = (pair_sum(3, r) + rel[1, q, :].astype(F32)).astype(BF16)
                return 0
            lax.fori_loop(0, HALF // CH, f, 0)
            send("fpU")

    def mm2(s):
        b, _, _ = where(s)

        def f(j, _):
            c = pl.ds(pl.multiple_of(j * 256, 256), 256)
            v = lax.dot_general(A[b], D.at[s][:, :, c].reshape(T, 256), NN, preferred_element_type=F32)
            if s == 0:
                acc[:, c] = v
            else:
                acc[:, c] += v
            return 0
        lax.fori_loop(0, C // 256, f, 0)

    def act_relay():
        got("aL+", "aU-")
        bl, br = (own + 6) % 8, (own + 2) % 8
        send("aR+", A.at[bl, LO], A.at[bl, LO], yp)
        send("aR-", A.at[br, HI], A.at[br, HI], ym)

    def act_pass():
        got("aU+", "aL-")
        bl, br = (own + 6) % 8, (own + 2) % 8
        send("ak1", A.at[bl], A.at[bl], kk)
        send("ak2", A.at[br], A.at[br], kk)

    def act_far():
        got("aR+", "aR-")
        bb = (own + 4) % 8
        send("ak3", A.at[bb], A.at[bb], kk)

    fwd_a(0)
    fwd_z(1)
    relay_x(0)
    act_relay()
    relayed_x(0)
    mm1(0)
    fwd_z(2)
    fwd_a(1)
    relay_x(1)
    stage2(0)
    act_pass()
    fwd_z(3)
    relayed_x(1)
    mm1(1)
    mm1(2)
    fwd_a(2)
    relay_x(2)
    stage2(1)
    stage2(2)
    fwd_z(4)
    act_far()
    relayed_x(2)
    mm1(3)
    mm1(4)
    fwd_a(3)
    relay_x(3)
    l_a.wait()
    got("ak0", "ak1", "ak2", "ak3")
    mm2(0)
    stage2(3)
    stage2(4)
    mm2(1)
    stage3(0)
    stage3(1)
    stage3(2)
    relayed_x(3)
    mm1(5)
    mm1(6)
    relay_x(4)
    mm2(2)
    stage2(5)
    stage2(6)
    stage3(3)
    stage3(4)
    fwd_a(4)
    relayed_x(4)
    mm1(7)
    Mx[0] = jnp.broadcast_to(jnp.max(mx[...].astype(F32)), (8, 128))
    send("mk", Mx.at[0], Mx.at[1], kk)
    mm2(3)
    stage2(7)
    got("mk")
    Mx[2] = jnp.maximum(Mx[0], Mx[1])
    send("m1", Mx.at[2], Mx.at[3], yp)
    send("m2", Mx.at[2], Mx.at[4], ym)
    send("m3", Mx.at[2], Mx.at[5], yy)
    mm2(4)
    stage3(5)
    stage3(6)
    mm2(5)
    mm2(6)
    stage3(7)
    mm2(7)
    got("m1", "m2", "m3")
    amax = jnp.maximum(jnp.maximum(Mx[2], Mx[3]), jnp.maximum(Mx[4], Mx[5]))
    gain = (peak_level / (amax + eps))[0:1, 0:1]
    factor = gain * scales[...]
    l_m.wait()
    outs = []
    for i in range(K // CH):
        r = pl.ds(i * CH, CH)
        acc[r, :] = mask_v[r, :].astype(F32) * factor * acc[r, :]
        c = pltpu.make_async_copy(acc.at[r], dlev_out.at[r], ls.at[4 + i])
        c.start()
        outs.append(c)
    got("fmU", "fmL", "fpL", "fpU")
    for i in range(K // CH):
        r = pl.ds(i * CH, CH)
        total = pair_sum(0, r) + fin[0, r, :].astype(F32) + fin[1, r, :].astype(F32)
        Cs[0, r, :] = total * gain
        c = pltpu.make_async_copy(Cs.at[0, r], din_out.at[r], ls.at[8 + i])
        c.start()
        outs.append(c)
    for c in outs:
        c.wait()
    some = {f"sib{s}" for s in range(8)}
    for n in ev:
        if n not in some:
            copy_of(n).wait_send()
    for s in range(8):
        b, mine, d = where(s)

        @pl.when(jnp.logical_not(mine))
        def _():
            copy_of(f"sib{s}").wait_send()


def on_device(activations, d_out, levels, scales, clip_mask):
    any_ = pl.BlockSpec(memory_space=pl.ANY)
    vm = pltpu.VMEM
    d_in_t, d_levels = pl.pallas_call(
        kernel,
        out_shape=(jax.ShapeDtypeStruct((K, T), F32), jax.ShapeDtypeStruct((K, C), F32)),
        in_specs=[any_, any_, any_, pl.BlockSpec(memory_space=vm), any_],
        out_specs=(any_, any_),
        scratch_shapes=[
            vm((8, 4, 128, C), BF16),
            vm((8, K, T), BF16),
            vm((K, C), BF16),
            vm((K, C), F32),
            vm((4, K, T), F32),
            vm((4, K, T), BF16),
            vm((4, K, T), BF16),
            vm((3, K, T), BF16),
            vm((2, HALF, T), BF16),
            vm((2, K, T), BF16),
            vm((K, C), BF16),
            vm((K, C), jnp.int32),
            vm((16, C), BF16),
            vm((6, 8, 128), F32),
            pltpu.SemaphoreType.DMA((N_EV,)),
            pltpu.SemaphoreType.DMA((N_EV,)),
            pltpu.SemaphoreType.DMA((12,)),
        ],
        compiler_params=pltpu.CompilerParams(
            collective_id=0, has_side_effects=True, vmem_limit_bytes=60 * 2**20),
        cost_estimate=pl.CostEstimate(flops=4 * 4096 * K * C, bytes_accessed=12 * 2**20, transcendentals=0),
        name="fused",
    )(activations.T, d_out, levels, scales.reshape(1, C), clip_mask)
    return d_in_t.T, d_levels


def solution(mesh):
    placed = (P("col", "row"), P("row", "col"), P("row", "col"), P("col"), P("row", "col"))
    return jax.shard_map(
        on_device,
        mesh=mesh,
        in_specs=placed,
        out_specs=(P("col", "row"), P("row", "col")),
        check_vma=False,
    )
```

time: 247 us -> 102 us (0.41); the launches traced: 244 us -> 102 us
  waiting for transfers between devices: 185 us -> 0 us
  Pallas kernels: 0 us -> 96.7 us
  matrix products: 26.6 us -> 0 us
  between operations: 14.5 us -> 0.65 us
  blocking collectives: 11.3 us -> 0 us
  other arithmetic: 6.03 us -> 0 us
  local copies, waits for them, and re-layouts: 0.01 us -> 4.68 us
    all_gather x2 -> x0, waiting for transfers between devices: 115 us -> none  [the longest x1 103 us: on_device(): lax.all_gather(d_out, 'row', axis=0, tiled=True).astype(jnp.float32)]
    pallas_call x0 -> x1, Pallas kernels: none -> 96.7 us  [on_device(): pl.pallas_call(kernel, out_shape=(jax.ShapeDtypeStruct((K, T), F32), jax....]
    reduce_scatter x1 -> x0, waiting for transfers between devices: 69.4 us -> none  [on_device(): lax.psum_scatter(lax.dot_general(grad_rows, dequant, (((1,), (1,)), ((),...]
    dot_general x2 -> x0, matrix products: 26.6 us -> none  [the longest x1 13.9 us: on_device(): lax.dot_general(grad_rows, dequant, (((1,), (1,)), ((), ())), preferred_e...]
    pmax x1 -> x0, blocking collectives: 11.3 us -> none  [on_device(): amax = lax.pmax(block_peak, 'col')]
    reduce_max x1 -> x0, other arithmetic: 6.03 us -> none  [on_device(): block_peak = jnp.max(jnp.abs(raw_all))]
    unnamed x6 -> x4, local copies, waits for them, and re-layouts: 0.01 us -> 4.68 us
  transfers between devices with their start and end apart: 3 -> 0, of which waited for: 3 -> 0; matrix products, arithmetic and copies ran while one was open for 13% -> 0% of each run, Pallas kernels for 0% -> 0%
where the time goes in v1:
time: 102 us
  Pallas kernels  96.7 us (95%)
  local copies, waits for them, and re-layouts  4.68 us (5%)
    pallas_call x1, Pallas kernels, on_device(): pl.pallas_call(kernel, out_shape=(jax.ShapeDtypeStruct((K, T), F32), jax....  96.7 us
    unnamed x4, local copies, waits for them, and re-layouts  4.68 us

profile of v1, /device:TPU:16, one launch (start us, length us, event | category | flops | bytes accessed | tf_op | source)
XLA Modules:
  0.0 102.0 jit_solution(3985121229729913642)
XLA Ops:
  0.6 96.7 %fused.1 = (f32[832,512]{1,0:T(8,128)}, f32[832,1024]{1,0:T(8,128)}) custom-call(bf16[832,512]{1,0:T(8,128)(2,1)} %bitcast.4, bf16[128,1024]{1,0:T(8,128)(2,1)} %dout.1, bf16[832,1024]{1,0:T(8,128)(2,1)} %levels.1, f32[1,1024]{1,0:T(1,128)} %bitcast.5, s32[832,1024]{1,0:T(8,128)} %mask.1), custom_call_target="tpu_custom_call" | custom-call | flops 13958643712 | bytes 12582912 | tf_op jit(solution)/shard_map/fused/pallas_call | solution.py:388
  97.3 0.0 copy-start
  97.3 2.9 %copy.9 = f32[512,832]{0,1:T(8,128)} copy(f32[512,832]{0,1:T(8,128)} %bitcast.3) | data formatting | bytes 3407872
  100.3 0.0 copy-done
  100.3 1.8 %copy.10 = f32[832,1024]{1,0:T(8,128)} copy(f32[832,1024]{1,0:T(8,128)S(1)} %copy-done) | data formatting | bytes 6815744
Async XLA Ops:
  97.3 2.9 %copy-start = (f32[832,1024]{1,0:T(8,128)S(1)}, f32[832,1024]{1,0:T(8,128)}, u32[]{:S(2)}) copy-start(f32[832,1024]{1,0:T(8,128)} %get-tuple-element.9) | copy-start | bytes 10223620

commit v2 on v1

v2 whole, which is shorter than its diff:
```python
import jax
import jax.numpy as jnp
from jax import lax
from jax.experimental import pallas as pl
from jax.experimental.pallas import tpu as pltpu
from jax.sharding import PartitionSpec as P

peak_level = 4.0
eps = 1e-06

MESH = pl.DeviceIdType.MESH
NT = (((1,), (1,)), ((), ()))
NN = (((1,), (0,)), ((), ()))
F32 = jnp.float32
BF16 = jnp.bfloat16

K = 832
T = 512
N = 256
C = 1024
XF = 48
HALF = K // 2
LO = pl.ds(0, HALF)
HI = pl.ds(HALF, HALF)
CH = 208
N_EV = 96

OFFS = (0, 1, 7, 2, 6, 3, 5, 4)


def up(h):
    return 2 * h - 1


def down(h):
    return 7 if h == 4 else 2 * h


def kernel(act, dout, levels, scales, mask, din, acc,
           D, A, W, Cs, Ssend, Srecv, Y, rel, fin, lev_v, mask_v, mx, Mx,
           ss, rs, ls):
    row, col = lax.axis_index("row"), lax.axis_index("col")
    z, x = row // 4, row % 4
    y, k = col // 2, col % 2

    def dev(dz=0, dx=0, dy=0, dk=0):
        return (((z + dz) % 8) * 4 + (x + dx) % 4, ((y + dy) % 4) * 2 + (k + dk) % 2)

    zp, zm, xp, xm = dev(dz=1), dev(dz=7), dev(dx=1), dev(dx=3)
    yp, ym, yy, kk = dev(dy=1), dev(dy=3), dev(dy=2), dev(dk=1)

    ev = {}

    def plan(name, src, dst, to):
        ev[name] = (len(ev), src, dst, to)

    def copy_of(name):
        i, src, dst, to = ev[name]
        return pltpu.make_async_remote_copy(
            src_ref=src, dst_ref=dst, send_sem=ss.at[i], recv_sem=rs.at[i],
            device_id=to, device_id_type=MESH)

    def send(name, *what):
        if what:
            plan(name, *what)
        copy_of(name).start()

    def got(*names):
        for n in names:
            copy_of(n).wait_recv()

    for p in range(2):
        plan(f"relL{p}", Y.at[2, p, LO], rel.at[0, p], yp)
        plan(f"relU{p}", Y.at[2, p, HI], rel.at[1, p], ym)
        plan(f"fmU{p}", Y.at[0, p, HI], fin.at[0, p, HI], yp)
        plan(f"fmL{p}", Y.at[0, p, LO], fin.at[0, p, LO], yp)
        plan(f"fpU{p}", Y.at[1, p, HI], fin.at[1, p, HI], ym)
        plan(f"fpL{p}", Y.at[1, p, LO], fin.at[1, p, LO], ym)
        for s in range(8):
            d = ((z + OFFS[s]) % 8 // 2 + 4 - y) % 4
            plan(f"sib{s}{p}", Ssend.at[d, p], Srecv.at[d, p], kk)
    xs = (x // 2 * 2, 2 - x // 2 * 2)

    own = 2 * y + k
    l_d = pltpu.make_async_copy(dout, D.at[0, x], ls.at[0])
    l_a = pltpu.make_async_copy(act, A.at[own], ls.at[1])
    l_w = pltpu.make_async_copy(levels, lev_v, ls.at[2])
    l_m = pltpu.make_async_copy(mask, mask_v, ls.at[3])

    barrier = pltpu.get_barrier_semaphore()
    peers = (zp, zm, xp, xm, yp, ym, yy, kk)
    for p in peers:
        pl.semaphore_signal(barrier, inc=1, device_id=p, device_id_type=MESH)
    l_d.start()
    l_w.start()
    l_a.start()
    pl.semaphore_wait(barrier, len(peers))

    a_rows, b_rows = pl.ds(0, XF), pl.ds(XF, 128 - XF)
    b_lo, b_hi = pl.ds(XF, 48), pl.ds(XF + 48, 80 - 48)

    send("xA+", dout.at[a_rows], D.at[0, x, a_rows], xp)
    send("xA-", dout.at[a_rows], D.at[0, x, a_rows], xm)
    send("zB+1", dout.at[b_rows], D.at[down(1), x, b_rows], zp)
    send("zB-1", dout.at[b_rows], D.at[up(1), x, b_rows], zm)
    send("aL+", act.at[LO], A.at[own, LO], yp)
    send("aU-", act.at[HI], A.at[own, HI], ym)
    send("xB+0", dout.at[b_rows], D.at[0, x, b_rows], xp)
    send("xB-0", dout.at[b_rows], D.at[0, x, b_rows], xm)
    send("aU+", act.at[HI], A.at[own, HI], yp)
    send("aL-", act.at[LO], A.at[own, LO], ym)
    send("ak0", act, A.at[own], kk)
    l_m.start()

    l_w.wait()

    def deq(i, _):
        r = pl.multiple_of(i * CH, 16)
        W[pl.ds(r, CH), :] = (lev_v[pl.ds(r, CH), :].astype(F32) * scales[...]).astype(BF16)
        return 0

    lax.fori_loop(0, K // CH, deq, 0)
    mx[...] = jnp.zeros_like(mx)
    l_d.wait()

    def fwd_z(h):
        got(f"zB+{h}", f"zB-{h}")
        if h < 3:
            send(f"zB+{h+1}", D.at[down(h), x, b_rows], D.at[down(h + 1), x, b_rows], zp)
            send(f"zB-{h+1}", D.at[up(h), x, b_rows], D.at[up(h + 1), x, b_rows], zm)
        if h == 3:
            send("zB+4", D.at[down(3), x, b_lo], D.at[7, x, b_lo], zp)
            send("zB-4", D.at[up(3), x, b_hi], D.at[7, x, b_hi], zm)

    def spread_x(h):
        pair = D.at[pl.ds(2 * h - 1, 2), x, b_rows] if h < 4 else D.at[7, x, b_rows]
        send(f"xB+{h}", pair, pair, xp)
        send(f"xB-{h}", pair, pair, xm)

    def fwd_a(h, p):
        if h == 0:
            if p == 0:
                got("xA+", "xA-")
            else:
                got("xR+", "xR-")
        elif h < 3:
            got(f"zA{p}+{h}", f"zA{p}-{h}")
        elif h == 3:
            got("zA0+3" if p == 0 else "zA1-3")
        else:
            got("zA0+4" if p == 0 else "zA1-4")
        if h == 4:
            return
        lo, hi = (0, 0) if h == 0 else (down(h), up(h))
        q = pl.ds(xs[p], 2)
        if h < 3 or p == 0:
            send(f"zA{p}+{h+1}", D.at[lo, q, a_rows], D.at[down(h + 1), q, a_rows], zp)
        if h < 3 or p == 1:
            send(f"zA{p}-{h+1}", D.at[hi, q, a_rows], D.at[up(h + 1) if h < 3 else 7, q, a_rows], zm)

    xl, xr = (x + 3) % 4, (x + 1) % 4

    def rest_a(p):
        got("zA0-3" if p == 0 else "zA1+3")

    def relay_a():
        r0, r1 = D.at[0, xl, pl.ds(0, 32)], D.at[0, xr, pl.ds(32, 16)]
        send("xR+", r0, r0, xp)
        send("xR-", r1, r1, xm)

    def relay_x(h):
        got(f"xB+{h}", f"xB-{h}")
        if h in (0, 4):
            s = 0 if h == 0 else 7
            r0, r1 = D.at[s, xl, b_lo], D.at[s, xr, b_hi]
        else:
            r0, r1 = D.at[up(h), xl, b_rows], D.at[down(h), xr, b_rows]
        send(f"xr+{h}", r0, r0, xp)
        send(f"xr-{h}", r1, r1, xm)

    def relayed_x(h):
        got(f"xr+{h}", f"xr-{h}")

    def where(s):
        b = (z + OFFS[s]) % 8
        return b, b % 2 == k, (b // 2 + 4 - y) % 4

    def mm1(s, p):
        b, mine, d = where(s)
        q = pl.ds(xs[p], 2)

        def part():
            return lax.dot_general(W[...], D[s, q].reshape(N, C), NT, preferred_element_type=F32)

        @pl.when(mine)
        def _():
            Cs[d, p] = part()

        @pl.when(jnp.logical_not(mine))
        def _():
            Ssend[d, p] = part().astype(BF16)
            send(f"sib{s}{p}")

        for j in range(2):
            def big(i, m):
                r = pl.multiple_of(i * 16, 16)
                return jnp.maximum(m, jnp.abs(D[s, xs[p] + j, pl.ds(r, 16), :]))

            mx[...] = lax.fori_loop(0, 8, big, mx[...], unroll=4)

    def rows_of(lo, n, fn):
        def body(i, _):
            fn(pl.ds(pl.multiple_of(lo + i * CH, 16), CH))
            return 0
        lax.fori_loop(0, n // CH, body, 0)

    def pair_sum(d, p, r):
        return Cs[d, p, r, :] + Srecv[d, p, r, :].astype(F32)

    def stage2(s, p):
        b, mine, d = where(s)

        @pl.when(mine)
        def _():
            got(f"sib{s}{p}")

            @pl.when(d == 2)
            def _():
                def f(r):
                    Y[2, p, r, :] = pair_sum(2, p, r).astype(BF16)
                rows_of(0, K, f)
                send(f"relL{p}")
                send(f"relU{p}")

            @pl.when(d == 1)
            def _():
                def f(r):
                    Y[0, p, r, :] = pair_sum(1, p, r).astype(BF16)
                rows_of(HALF, HALF, f)
                send(f"fmU{p}")

            @pl.when(d == 3)
            def _():
                def f(r):
                    Y[1, p, r, :] = pair_sum(3, p, r).astype(BF16)
                rows_of(0, HALF, f)
                send(f"fpL{p}")

    def stage3(s, p):
        b, mine, d = where(s)

        @pl.when(jnp.logical_and(mine, d == 1))
        def _():
            got(f"relL{p}")

            def f(r):
                Y[0, p, r, :] = (pair_sum(1, p, r) + rel[0, p, r, :].astype(F32)).astype(BF16)
            rows_of(0, HALF, f)
            send(f"fmL{p}")

        @pl.when(jnp.logical_and(mine, d == 3))
        def _():
            got(f"relU{p}")

            def f(i, _):
                r = pl.ds(pl.multiple_of(HALF + i * CH, 16), CH)
                q = pl.ds(pl.multiple_of(i * CH, 16), CH)
                Y[1, p, r, :] = (pair_sum(3, p, r) + rel[1, p, q, :].astype(F32)).astype(BF16)
                return 0
            lax.fori_loop(0, HALF // CH, f, 0)
            send(f"fpU{p}")

    def mm2(s):
        b, _, _ = where(s)

        def f(j, _):
            c = pl.ds(pl.multiple_of(j * 256, 256), 256)
            v = lax.dot_general(A[b], D.at[s][:, :, c].reshape(T, 256), NN, preferred_element_type=F32)
            if s == 0:
                acc[:, c] = v
            else:
                acc[:, c] += v
            return 0
        lax.fori_loop(0, C // 256, f, 0)

    def act_relay():
        got("aL+", "aU-")
        bl, br = (own + 6) % 8, (own + 2) % 8
        send("aR+", A.at[bl, LO], A.at[bl, LO], yp)
        send("aR-", A.at[br, HI], A.at[br, HI], ym)

    def act_pass():
        got("aU+", "aL-")
        bl, br = (own + 6) % 8, (own + 2) % 8
        send("ak1", A.at[bl], A.at[bl], kk)
        send("ak2", A.at[br], A.at[br], kk)

    def act_far():
        got("aR+", "aR-")
        bb = (own + 4) % 8
        send("ak3", A.at[bb], A.at[bb], kk)

    fwd_a(0, 0)
    relay_a()
    fwd_z(1)
    spread_x(1)
    relay_x(0)
    mm1(0, 0)
    fwd_a(1, 0)
    act_relay()
    fwd_z(2)
    spread_x(2)
    fwd_a(0, 1)
    relay_x(1)
    mm1(1, 0)
    mm1(2, 0)
    fwd_a(2, 0)
    relayed_x(0)
    mm1(0, 1)
    stage2(0, 0)
    act_pass()
    fwd_z(3)
    spread_x(3)
    stage2(1, 0)
    stage2(2, 0)
    relay_x(2)
    fwd_a(1, 1)
    mm1(3, 0)
    mm1(4, 0)
    stage2(0, 1)
    relayed_x(1)
    mm1(1, 1)
    mm1(2, 1)
    act_far()
    fwd_a(3, 0)
    stage2(3, 0)
    stage2(4, 0)
    fwd_z(4)
    spread_x(4)
    l_a.wait()
    got("ak0", "ak1", "ak2", "ak3")
    mm2(0)
    relay_x(3)
    fwd_a(2, 1)
    rest_a(0)
    mm1(5, 0)
    mm1(6, 0)
    stage2(1, 1)
    stage2(2, 1)
    relayed_x(2)
    mm1(3, 1)
    mm1(4, 1)
    fwd_a(3, 1)
    stage2(5, 0)
    stage2(6, 0)
    stage3(0, 0)
    stage3(1, 0)
    stage3(2, 0)
    relay_x(4)
    fwd_a(4, 0)
    mm1(7, 0)
    stage3(0, 1)
    stage2(3, 1)
    stage2(4, 1)
    stage3(3, 0)
    stage3(4, 0)
    mm2(1)
    stage2(7, 0)
    stage3(1, 1)
    stage3(2, 1)
    relayed_x(3)
    rest_a(1)
    mm1(5, 1)
    mm1(6, 1)
    relayed_x(4)
    fwd_a(4, 1)
    mm1(7, 1)
    Mx[0] = jnp.broadcast_to(jnp.max(mx[...].astype(F32)), (8, 128))
    send("mk", Mx.at[0], Mx.at[1], kk)
    stage2(5, 1)
    stage2(6, 1)
    stage3(5, 0)
    stage3(6, 0)
    stage2(7, 1)
    got("mk")
    Mx[2] = jnp.maximum(Mx[0], Mx[1])
    send("m1", Mx.at[2], Mx.at[3], yp)
    send("m2", Mx.at[2], Mx.at[4], ym)
    send("m3", Mx.at[2], Mx.at[5], yy)
    stage3(3, 1)
    stage3(4, 1)
    stage3(7, 0)
    mm2(2)
    mm2(3)
    stage3(5, 1)
    stage3(6, 1)
    mm2(4)
    stage3(7, 1)
    mm2(5)
    mm2(6)
    mm2(7)
    got("m1", "m2", "m3")
    amax = jnp.maximum(jnp.maximum(Mx[2], Mx[3]), jnp.maximum(Mx[4], Mx[5]))
    gain = (peak_level / (amax + eps))[0:1, 0:1]
    factor = gain * scales[...]
    l_m.wait()
    for i in range(K // CH):
        r = pl.ds(i * CH, CH)
        acc[r, :] = mask_v[r, :].astype(F32) * factor * acc[r, :]
    for p in range(2):
        got(f"fmU{p}", f"fmL{p}", f"fpL{p}", f"fpU{p}")
        for i in range(2):
            r = pl.ds(i * HALF, HALF)
            total = pair_sum(0, p, r) + fin[0, p, r, :].astype(F32) + fin[1, p, r, :].astype(F32)
            din[xs[p] // 2, r, :] = total * gain
    for n in ev:
        if n[:3] != "sib":
            copy_of(n).wait_send()
    for s in range(8):
        b, mine, d = where(s)

        @pl.when(jnp.logical_not(mine))
        def _():
            for p in range(2):
                copy_of(f"sib{s}{p}").wait_send()


def on_device(activations, d_out, levels, scales, clip_mask):
    any_ = pl.BlockSpec(memory_space=pl.ANY)
    vm = pltpu.VMEM
    d_in_t, d_levels = pl.pallas_call(
        kernel,
        out_shape=(pltpu.VMEM((2, K, N), F32), pltpu.VMEM((K, C), F32)),
        in_specs=[any_, any_, any_, pl.BlockSpec(memory_space=vm), any_],
        out_specs=(pl.BlockSpec(memory_space=vm), pl.BlockSpec(memory_space=vm)),
        scratch_shapes=[
            vm((8, 4, 128, C), BF16),
            vm((8, K, T), BF16),
            vm((K, C), BF16),
            vm((4, 2, K, N), F32),
            vm((4, 2, K, N), BF16),
            vm((4, 2, K, N), BF16),
            vm((3, 2, K, N), BF16),
            vm((2, 2, HALF, N), BF16),
            vm((2, 2, K, N), BF16),
            vm((K, C), BF16),
            vm((K, C), jnp.int32),
            vm((16, C), BF16),
            vm((6, 8, 128), F32),
            pltpu.SemaphoreType.DMA((N_EV,)),
            pltpu.SemaphoreType.DMA((N_EV,)),
            pltpu.SemaphoreType.DMA((12,)),
        ],
        compiler_params=pltpu.CompilerParams(
            collective_id=0, has_side_effects=True, vmem_limit_bytes=50 * 2**20),
        cost_estimate=pl.CostEstimate(flops=4 * 4096 * K * C, bytes_accessed=12 * 2**20, transcendentals=0),
        name="fused",
    )(activations.T, d_out, levels, scales.reshape(1, C), clip_mask)
    return d_in_t.transpose(0, 2, 1).reshape(T, K), d_levels


def solution(mesh):
    placed = (P("col", "row"), P("row", "col"), P("row", "col"), P("col"), P("row", "col"))
    return jax.shard_map(
        on_device,
        mesh=mesh,
        in_specs=placed,
        out_specs=(P("col", "row"), P("row", "col")),
        check_vma=False,
    )
```

time: 102 us -> 84.7 us (0.83)
  Pallas kernels: 96.7 us -> 80.3 us
  local copies, waits for them, and re-layouts: 4.68 us -> 3.19 us
    pallas_call x1, Pallas kernels: 96.7 us -> 80.3 us  [on_device(): pl.pallas_call(kernel, out_shape=(pltpu.VMEM((2, K, N), F32), pltpu.VMEM(...]
    unnamed x4 -> x1, local copies, waits for them, and re-layouts: 4.68 us -> 1.75 us
    reshape x0 -> x1, local copies, waits for them, and re-layouts: none -> 1.45 us  [on_device(): return (d_in_t.transpose(0, 2, 1).reshape(T, K), d_levels)]
where the time goes in v2:
time: 84.7 us; the launch traced here: 84.1 us
  Pallas kernels  80.3 us (95%)
  local copies, waits for them, and re-layouts  3.19 us (4%)
    pallas_call x1, Pallas kernels, on_device(): pl.pallas_call(kernel, out_shape=(pltpu.VMEM((2, K, N), F32), pltpu.VMEM(...  80.3 us
    unnamed x1, local copies, waits for them, and re-layouts  1.75 us

profile of v2, /device:TPU:16, one launch (start us, length us, event | category | flops | bytes accessed | tf_op | source)
XLA Modules:
  0.0 84.1 jit_solution(13385925776039196608)
XLA Ops:
  0.6 80.3 %fused.1 = (f32[2,832,256]{2,1,0:T(8,128)S(1)}, f32[832,1024]{1,0:T(8,128)S(1)}) custom-call(bf16[832,512]{1,0:T(8,128)(2,1)} %bitcast.7, bf16[128,1024]{1,0:T(8,128)(2,1)} %dout.1, bf16[832,1024]{1,0:T(8,128)(2,1)} %levels.1, f32[1,1024]{1,0:T(1,128)} %bitcast.8, s32[832,1024]{1,0:T(8,128)} %mask.1), custom_call_target="tpu_custom_call" | custom-call | flops 13958643712 | bytes 12582912 | tf_op jit(solution)/shard_map/fused/pallas_call | solution.py:431
  80.9 1.4 %copy.8 = f32[2,104,8,256]{3,2,0,1:T(8,128)} copy(f32[2,104,8,256]{3,2,1,0:T(8,128)S(1)} %bitcast.5) | data formatting | bytes 3407872 | tf_op jit(solution)/shard_map/reshape | solution.py:459
  82.4 1.7 %copy.10 = f32[832,1024]{1,0:T(8,128)} copy(f32[832,1024]{1,0:T(8,128)S(1)} %get-tuple-element.7) | data formatting | bytes 6815744

commit v3 on v2

--- a/solution.py
+++ b/solution.py
@@ -103,25 +103,37 @@
     send("xA-", dout.at[a_rows], D.at[0, x, a_rows], xm)
     send("zB+1", dout.at[b_rows], D.at[down(1), x, b_rows], zp)
     send("zB-1", dout.at[b_rows], D.at[up(1), x, b_rows], zm)
-    send("aL+", act.at[LO], A.at[own, LO], yp)
-    send("aU-", act.at[HI], A.at[own, HI], ym)
-    send("xB+0", dout.at[b_rows], D.at[0, x, b_rows], xp)
-    send("xB-0", dout.at[b_rows], D.at[0, x, b_rows], xm)
-    send("aU+", act.at[HI], A.at[own, HI], yp)
-    send("aL-", act.at[LO], A.at[own, LO], ym)
-    send("ak0", act, A.at[own], kk)
     l_m.start()
-
-    l_w.wait()
-
-    def deq(i, _):
-        r = pl.multiple_of(i * CH, 16)
-        W[pl.ds(r, CH), :] = (lev_v[pl.ds(r, CH), :].astype(F32) * scales[...]).astype(BF16)
-        return 0
-
-    lax.fori_loop(0, K // CH, deq, 0)
     mx[...] = jnp.zeros_like(mx)
-    l_d.wait()
+
+    def start_x():
+        send("xB+0", dout.at[b_rows], D.at[0, x, b_rows], xp)
+        send("xB-0", dout.at[b_rows], D.at[0, x, b_rows], xm)
+
+    def start_act1():
+        send("aL+", act.at[LO], A.at[own, LO], yp)
+        send("aU-", act.at[HI], A.at[own, HI], ym)
+
+    def start_act2():
+        send("aU+", act.at[HI], A.at[own, HI], yp)
+        send("aL-", act.at[LO], A.at[own, LO], ym)
+
+    def start_pair():
+        send("ak0", act, A.at[own], kk)
+
+    def deq():
+        l_w.wait()
+
+        def f(r):
+            W[r, :] = (lev_v[r, :].astype(F32) * scales[...]).astype(BF16)
+        rows_of(0, K, f)
+        l_d.wait()
+
+    def rows_of(lo, n, fn):
+        def body(i, _):
+            fn(pl.ds(pl.multiple_of(lo + i * CH, 16), CH))
+            return 0
+        lax.fori_loop(0, n // CH, body, 0)
 
     def fwd_z(h):
         got(f"zB+{h}", f"zB-{h}")
@@ -137,49 +149,44 @@
         send(f"xB+{h}", pair, pair, xp)
         send(f"xB-{h}", pair, pair, xm)
 
-    def fwd_a(h, p):
-        if h == 0:
-            if p == 0:
-                got("xA+", "xA-")
-            else:
-                got("xR+", "xR-")
-        elif h < 3:
-            got(f"zA{p}+{h}", f"zA{p}-{h}")
-        elif h == 3:
-            got("zA0+3" if p == 0 else "zA1-3")
-        else:
-            got("zA0+4" if p == 0 else "zA1-4")
-        if h == 4:
-            return
-        lo, hi = (0, 0) if h == 0 else (down(h), up(h))
+    def fa(way, h, p):
+        if h > 0:
+            got(f"zA{p}{way}{h}")
+        s = 0 if h == 0 else down(h) if way == "+" else up(h)
+        to = down(h + 1) if way == "+" or h == 3 else up(h + 1)
         q = pl.ds(xs[p], 2)
-        if h < 3 or p == 0:
-            send(f"zA{p}+{h+1}", D.at[lo, q, a_rows], D.at[down(h + 1), q, a_rows], zp)
-        if h < 3 or p == 1:
-            send(f"zA{p}-{h+1}", D.at[hi, q, a_rows], D.at[up(h + 1) if h < 3 else 7, q, a_rows], zm)
+        send(f"zA{p}{way}{h+1}", D.at[s, q, a_rows], D.at[to, q, a_rows], zp if way == "+" else zm)
+
+    def ea(way, h, p):
+        got(f"zA{p}{way}{h}")
 
     xl, xr = (x + 3) % 4, (x + 1) % 4
 
-    def rest_a(p):
-        got("zA0-3" if p == 0 else "zA1+3")
-
     def relay_a():
+        got("xA+", "xA-")
         r0, r1 = D.at[0, xl, pl.ds(0, 32)], D.at[0, xr, pl.ds(32, 16)]
         send("xR+", r0, r0, xp)
         send("xR-", r1, r1, xm)
 
-    def relay_x(h):
+    def got_a():
+        got("xR+", "xR-")
+
+    def got_x(h):
         got(f"xB+{h}", f"xB-{h}")
-        if h in (0, 4):
-            s = 0 if h == 0 else 7
-            r0, r1 = D.at[s, xl, b_lo], D.at[s, xr, b_hi]
-        else:
-            r0, r1 = D.at[up(h), xl, b_rows], D.at[down(h), xr, b_rows]
-        send(f"xr+{h}", r0, r0, xp)
-        send(f"xr-{h}", r1, r1, xm)
-
-    def relayed_x(h):
-        got(f"xr+{h}", f"xr-{h}")
+
+    def relay_p(h):
+        r = D.at[0 if h == 0 else 7, xl, b_lo] if h in (0, 4) else D.at[up(h), xl, b_rows]
+        send(f"xr+{h}", r, r, xp)
+
+    def relay_m(h):
+        r = D.at[0 if h == 0 else 7, xr, b_hi] if h in (0, 4) else D.at[down(h), xr, b_rows]
+        send(f"xr-{h}", r, r, xm)
+
+    def got_p(h):
+        got(f"xr+{h}")
+
+    def got_m(h):
+        got(f"xr-{h}")
 
     def where(s):
         b = (z + OFFS[s]) % 8
@@ -207,12 +214,6 @@
                 return jnp.maximum(m, jnp.abs(D[s, xs[p] + j, pl.ds(r, 16), :]))
 
             mx[...] = lax.fori_loop(0, 8, big, mx[...], unroll=4)
-
-    def rows_of(lo, n, fn):
-        def body(i, _):
-            fn(pl.ds(pl.multiple_of(lo + i * CH, 16), CH))
-            return 0
-        lax.fori_loop(0, n // CH, body, 0)
 
     def pair_sum(d, p, r):
         return Cs[d, p, r, :] + Srecv[d, p, r, :].astype(F32)
@@ -270,18 +271,55 @@
             lax.fori_loop(0, HALF // CH, f, 0)
             send(f"fpU{p}")
 
-    def mm2(s):
-        b, _, _ = where(s)
-
-        def f(j, _):
-            c = pl.ds(pl.multiple_of(j * 256, 256), 256)
-            v = lax.dot_general(A[b], D.at[s][:, :, c].reshape(T, 256), NN, preferred_element_type=F32)
-            if s == 0:
+    def block(s, j):
+        return lax.dot_general(A[where(s)[0]], D.at[s][:, :, pl.ds(j * 256, 256)].reshape(T, 256),
+                               NN, preferred_element_type=F32)
+
+    def mm2(*slots):
+        for j in range(C // 256):
+            v = block(slots[0], j)
+            for s in slots[1:]:
+                v = v + block(s, j)
+            c = pl.ds(j * 256, 256)
+            if slots[0] == 0:
                 acc[:, c] = v
             else:
                 acc[:, c] += v
-            return 0
-        lax.fori_loop(0, C // 256, f, 0)
+
+    def mm2_last():
+        l_m.wait()
+        factor = gain() * scales[...]
+        for j in range(C // 256):
+            c = pl.ds(j * 256, 256)
+            acc[:, c] = (acc[:, c] + block(7, j)) * (mask_v[:, c].astype(F32) * factor[:, j * 256:(j + 1) * 256])
+
+    def gain():
+        amax = jnp.maximum(jnp.maximum(Mx[2], Mx[3]), jnp.maximum(Mx[4], Mx[5]))
+        return (peak_level / (amax + eps))[0:1, 0:1]
+
+    def peak_pair():
+        Mx[0] = jnp.broadcast_to(jnp.max(mx[...].astype(F32)), (8, 128))
+        send("mk", Mx.at[0], Mx.at[1], kk)
+
+    def peak_col():
+        got("mk")
+        Mx[2] = jnp.maximum(Mx[0], Mx[1])
+        send("m1", Mx.at[2], Mx.at[3], yp)
+        send("m2", Mx.at[2], Mx.at[4], ym)
+        send("m3", Mx.at[2], Mx.at[5], yy)
+
+    def act_all():
+        l_a.wait()
+        got("ak0", "ak1", "ak2", "ak3")
+
+    def finish(p):
+        got(f"fmU{p}", f"fmL{p}", f"fpL{p}", f"fpU{p}")
+        g = gain()
+
+        def f(r):
+            total = pair_sum(0, p, r) + fin[0, p, r, :].astype(F32) + fin[1, p, r, :].astype(F32)
+            din[xs[p] // 2, r, :] = total * g
+        rows_of(0, K, f)
 
     def act_relay():
         got("aL+", "aU-")
@@ -300,119 +338,126 @@
         bb = (own + 4) % 8
         send("ak3", A.at[bb], A.at[bb], kk)
 
-    fwd_a(0, 0)
+    start_act1()
+    start_x()
+    start_act2()
+    deq()
     relay_a()
+    fa("+", 0, 0)
+    fa("-", 0, 0)
+    start_pair()
     fwd_z(1)
     spread_x(1)
-    relay_x(0)
-    mm1(0, 0)
-    fwd_a(1, 0)
-    act_relay()
+    fa("-", 1, 0)
+    got_x(0)
+    fa("+", 1, 0)
     fwd_z(2)
     spread_x(2)
-    fwd_a(0, 1)
-    relay_x(1)
+    mm1(0, 0)
+    got_x(1)
     mm1(1, 0)
+    got_a()
+    fa("+", 2, 0)
+    fa("-", 2, 0)
+    act_relay()
     mm1(2, 0)
-    fwd_a(2, 0)
-    relayed_x(0)
-    mm1(0, 1)
-    stage2(0, 0)
-    act_pass()
     fwd_z(3)
     spread_x(3)
+    got_x(2)
+    fa("+", 0, 1)
+    fa("-", 0, 1)
+    mm1(4, 0)
     stage2(1, 0)
+    act_pass()
+    fwd_z(4)
+    stage2(4, 0)
+    spread_x(4)
+    mm1(3, 0)
+    relay_m(0)
+    stage2(0, 0)
+    act_far()
+    relay_p(0)
+    fa("+", 3, 0)
+    got_x(3)
+    ea("-", 3, 0)
+    relay_p(1)
+    relay_m(1)
+    fa("-", 1, 1)
+    mm1(5, 0)
+    relay_p(2)
+    stage2(3, 0)
+    mm1(6, 0)
+    relay_p(3)
     stage2(2, 0)
-    relay_x(2)
-    fwd_a(1, 1)
-    mm1(3, 0)
-    mm1(4, 0)
+    act_all()
+    fa("+", 1, 1)
+    ea("+", 4, 0)
+    got_m(0)
+    got_x(4)
+    stage2(6, 0)
+    relay_m(2)
+    stage2(5, 0)
+    relay_m(3)
+    got_p(0)
+    mm1(7, 0)
+    relay_m(4)
+    mm1(0, 1)
+    stage3(2, 0)
+    fa("-", 2, 1)
+    relay_p(4)
+    fa("+", 2, 1)
+    got_m(1)
+    got_p(1)
+    mm1(2, 1)
+    stage2(7, 0)
+    mm2(0)
+    mm1(1, 1)
+    got_p(2)
+    stage3(1, 0)
+    fa("-", 3, 1)
+    mm1(3, 1)
+    stage3(4, 0)
+    got_m(2)
+    stage3(3, 0)
     stage2(0, 1)
-    relayed_x(1)
-    mm1(1, 1)
-    mm1(2, 1)
-    act_far()
-    fwd_a(3, 0)
-    stage2(3, 0)
-    stage2(4, 0)
-    fwd_z(4)
-    spread_x(4)
-    l_a.wait()
-    got("ak0", "ak1", "ak2", "ak3")
-    mm2(0)
-    relay_x(3)
-    fwd_a(2, 1)
-    rest_a(0)
-    mm1(5, 0)
-    mm1(6, 0)
+    mm1(4, 1)
+    got_m(3)
+    stage2(2, 1)
     stage2(1, 1)
-    stage2(2, 1)
-    relayed_x(2)
-    mm1(3, 1)
-    mm1(4, 1)
-    fwd_a(3, 1)
-    stage2(5, 0)
-    stage2(6, 0)
     stage3(0, 0)
-    stage3(1, 0)
-    stage3(2, 0)
-    relay_x(4)
-    fwd_a(4, 0)
-    mm1(7, 0)
-    stage3(0, 1)
-    stage2(3, 1)
-    stage2(4, 1)
-    stage3(3, 0)
-    stage3(4, 0)
-    mm2(1)
-    stage2(7, 0)
-    stage3(1, 1)
-    stage3(2, 1)
-    relayed_x(3)
-    rest_a(1)
+    stage3(5, 0)
+    got_p(3)
+    ea("+", 3, 1)
+    stage3(7, 0)
     mm1(5, 1)
     mm1(6, 1)
-    relayed_x(4)
-    fwd_a(4, 1)
+    stage2(3, 1)
+    got_m(4)
+    stage3(6, 0)
+    stage2(4, 1)
+    got_p(4)
+    ea("-", 4, 1)
     mm1(7, 1)
-    Mx[0] = jnp.broadcast_to(jnp.max(mx[...].astype(F32)), (8, 128))
-    send("mk", Mx.at[0], Mx.at[1], kk)
+    stage2(6, 1)
+    peak_pair()
+    mm2(5, 6)
     stage2(5, 1)
-    stage2(6, 1)
-    stage3(5, 0)
-    stage3(6, 0)
     stage2(7, 1)
-    got("mk")
-    Mx[2] = jnp.maximum(Mx[0], Mx[1])
-    send("m1", Mx.at[2], Mx.at[3], yp)
-    send("m2", Mx.at[2], Mx.at[4], ym)
-    send("m3", Mx.at[2], Mx.at[5], yy)
+    stage3(2, 1)
+    mm2(3, 4)
+    peak_col()
+    stage3(0, 1)
+    stage3(1, 1)
     stage3(3, 1)
     stage3(4, 1)
-    stage3(7, 0)
-    mm2(2)
-    mm2(3)
+    mm2(1, 2)
+    stage3(7, 1)
+    stage3(6, 1)
+    got("m1", "m2", "m3")
+    finish(0)
     stage3(5, 1)
-    stage3(6, 1)
-    mm2(4)
-    stage3(7, 1)
-    mm2(5)
-    mm2(6)
-    mm2(7)
-    got("m1", "m2", "m3")
-    amax = jnp.maximum(jnp.maximum(Mx[2], Mx[3]), jnp.maximum(Mx[4], Mx[5]))
-    gain = (peak_level / (amax + eps))[0:1, 0:1]
-    factor = gain * scales[...]
-    l_m.wait()
-    for i in range(K // CH):
-        r = pl.ds(i * CH, CH)
-        acc[r, :] = mask_v[r, :].astype(F32) * factor * acc[r, :]
-    for p in range(2):
-        got(f"fmU{p}", f"fmL{p}", f"fpL{p}", f"fpU{p}")
-        for i in range(2):
-            r = pl.ds(i * HALF, HALF)
-            total = pair_sum(0, p, r) + fin[0, p, r, :].astype(F32) + fin[1, p, r, :].astype(F32)
-            din[xs[p] // 2, r, :] = total * gain
+    mm2_last()
+    finish(1)
     for n in ev:
         if n[:3] != "sib":
             copy_of(n).wait_send()
@@ -423,6 +468,17 @@
         def _():
             for p in range(2):
                 copy_of(f"sib{s}{p}").wait_send()
+
+
+def store(din, dlev, din_out, dlev_out, sems):
+    copies = [pltpu.make_async_copy(din.at[p], din_out.at[:, pl.ds(p * N, N)], sems.at[p]) for p in range(2)]
+    for i in range(4):
+        r = pl.ds(i * CH, CH)
+        copies.append(pltpu.make_async_copy(dlev.at[r], dlev_out.at[r], sems.at[2 + i]))
+    for c in copies:
+        c.start()
+    for c in copies:
+        c.wait()
 
 
 def on_device(activations, d_out, levels, scales, clip_mask):
@@ -456,7 +512,18 @@
         cost_estimate=pl.CostEstimate(flops=4 * 4096 * K * C, bytes_accessed=12 * 2**20, transcendentals=0),
         name="fused",
     )(activations.T, d_out, levels, scales.reshape(1, C), clip_mask)
-    return d_in_t.transpose(0, 2, 1).reshape(T, K), d_levels
+    d_in_t = pltpu.with_memory_space_constraint(d_in_t, vm)
+    d_levels = pltpu.with_memory_space_constraint(d_levels, vm)
+    d_in_t, d_levels = pl.pallas_call(
+        store,
+        out_shape=(jax.ShapeDtypeStruct((K, T), F32), jax.ShapeDtypeStruct((K, C), F32)),
+        in_specs=[pl.BlockSpec(memory_space=vm)] * 2,
+        out_specs=(any_, any_),
+        scratch_shapes=[pltpu.SemaphoreType.DMA((6,))],
+        compiler_params=pltpu.CompilerParams(vmem_limit_bytes=8 * 2**20),
+        name="store",
+    )(d_in_t, d_levels)
+    return d_in_t.T, d_levels
 
 
 def solution(mesh):

time: 84.7 us -> 83.4 us (0.985)
  local copies, waits for them, and re-layouts: 3.19 us -> 0 us
  Pallas kernels: 80.3 us -> 81.9 us
    pallas_call x0 -> x1, Pallas kernels: none -> 2.36 us  [on_device(): pl.pallas_call(store, out_shape=(jax.ShapeDtypeStruct((K, T), F32), jax.S...]
    unnamed x1 -> x0, local copies, waits for them, and re-layouts: 1.75 us -> none
    reshape x1 -> x0, local copies, waits for them, and re-layouts: 1.45 us -> none  [on_device(): return (d_in_t.transpose(0, 2, 1).reshape(T, K), d_levels)]
where the time goes in v3:
time: 83.4 us; the launch traced here: 82.7 us
  Pallas kernels  81.9 us (98%)
    pallas_call x1, Pallas kernels, on_device(): pl.pallas_call(kernel, out_shape=(pltpu.VMEM((2, K, N), F32), pltpu.VMEM(...  79.5 us
    pallas_call x1, Pallas kernels, on_device(): pl.pallas_call(store, out_shape=(jax.ShapeDtypeStruct((K, T), F32), jax.S...  2.36 us

profile of v3, /device:TPU:16, one launch (start us, length us, event | category | flops | bytes accessed | tf_op | source)
XLA Modules:
  0.0 82.7 jit_solution(11988888436051005431)
XLA Ops:
  0.6 79.5 %fused.1 = (f32[2,832,256]{2,1,0:T(8,128)S(1)}, f32[832,1024]{1,0:T(8,128)S(1)}) custom-call(bf16[832,512]{1,0:T(8,128)(2,1)} %bitcast.4, bf16[128,1024]{1,0:T(8,128)(2,1)} %dout.1, bf16[832,1024]{1,0:T(8,128)(2,1)} %levels.1, f32[1,1024]{1,0:T(1,128)} %bitcast.5, s32[832,1024]{1,0:T(8,128)} %mask.1), custom_call_target="tpu_custom_call" | custom-call | flops 13958643712 | bytes 12582912 | tf_op jit(solution)/shard_map/fused/pallas_call | solution.py:487
  80.2 2.4 %store.1 = (f32[832,512]{1,0:T(8,128)}, f32[832,1024]{1,0:T(8,128)}) custom-call(f32[2,832,256]{2,1,0:T(8,128)S(1)} %get-tuple-element.6.din, f32[832,1024]{1,0:T(8,128)S(1)} %get-tuple-element.7.dlev), custom_call_target="tpu_custom_call" | custom-call | tf_op jit(solution)/shard_map/store/pallas_call | solution.py:517

commit v4 on v3

--- a/solution.py
+++ b/solution.py
@@ -438,10 +438,10 @@
     got_p(4)
     ea("-", 4, 1)
     mm1(7, 1)
+    stage2(5, 1)
     stage2(6, 1)
     peak_pair()
     mm2(5, 6)
-    stage2(5, 1)
     stage2(7, 1)
     stage3(2, 1)
     mm2(3, 4)
@@ -451,11 +451,11 @@
     stage3(3, 1)
     stage3(4, 1)
     mm2(1, 2)
+    stage3(5, 1)
+    stage3(6, 1)
     stage3(7, 1)
-    stage3(6, 1)
     got("m1", "m2", "m3")
     finish(0)
-    stage3(5, 1)
     mm2_last()
     finish(1)
     for n in ev:

time: 83.4 us -> 82.8 us (level)
  no operation moved by 1% of the time
where the time goes in v4:
time: 82.8 us; the launch traced here: 82.7 us
  Pallas kernels  81.9 us (99%)
    pallas_call x1, Pallas kernels, on_device(): pl.pallas_call(kernel, out_shape=(pltpu.VMEM((2, K, N), F32), pltpu.VMEM(...  79.5 us
    pallas_call x1, Pallas kernels, on_device(): pl.pallas_call(store, out_shape=(jax.ShapeDtypeStruct((K, T), F32), jax.S...  2.36 us

profile of v4, /device:TPU:16, one launch (start us, length us, event | category | flops | bytes accessed | tf_op | source)
XLA Modules:
  0.0 82.7 jit_solution(7780258484920472970)
XLA Ops:
  0.6 79.5 %fused.1 = (f32[2,832,256]{2,1,0:T(8,128)S(1)}, f32[832,1024]{1,0:T(8,128)S(1)}) custom-call(bf16[832,512]{1,0:T(8,128)(2,1)} %bitcast.4, bf16[128,1024]{1,0:T(8,128)(2,1)} %dout.1, bf16[832,1024]{1,0:T(8,128)(2,1)} %levels.1, f32[1,1024]{1,0:T(1,128)} %bitcast.5, s32[832,1024]{1,0:T(8,128)} %mask.1), custom_call_target="tpu_custom_call" | custom-call | flops 13958643712 | bytes 12582912 | tf_op jit(solution)/shard_map/fused/pallas_call | solution.py:487
  80.2 2.4 %store.1 = (f32[832,512]{1,0:T(8,128)}, f32[832,1024]{1,0:T(8,128)}) custom-call(f32[2,832,256]{2,1,0:T(8,128)S(1)} %get-tuple-element.6.din, f32[832,1024]{1,0:T(8,128)S(1)} %get-tuple-element.7.dlev), custom_call_target="tpu_custom_call" | custom-call | tf_op jit(solution)/shard_map/store/pallas_call | solution.py:517
